TPU v7x, 32 devices: a whole 2x2x4 slice. The times are simulated.
32 devices in a mesh: ctx: 8 (over z, y), chan: 4 (over x, core).
Axes of the slice: x: 2, y: 2, z: 4, core: 2. Of those that a mesh axis runs over, the one named last changes fastest.
Arguments:
- query: bfloat16 [1, 1024, 8192], P(None, 'ctx', 'chan'), may hold values from -6 to 6
- key_in: bfloat16 [1, 1024, 8192], P(None, 'ctx', 'chan'), may hold values from -6 to 6
- value_in: bfloat16 [1, 1024, 8192], P(None, 'ctx', 'chan'), may hold values from -6 to 6
- cotangent: bfloat16 [1, 1024, 8192], P(None, 'ctx', 'chan'), may hold values from -6 to 6
- filters: float32 [512, 128], P('chan'), may hold values from -0.5 to 0.5
- norm_gain: float32 [8192], P('chan'), may hold values from 0.1 to 1.9
Outputs:
- normed: bfloat16 [1, 1024, 8192], P(None, 'ctx', 'chan')
- grad_query: bfloat16 [1, 1024, 8192], P(None, 'ctx', 'chan')
- grad_key: bfloat16 [1, 1024, 8192], P(None, 'ctx', 'chan')
- grad_value: bfloat16 [1, 1024, 8192], P(None, 'ctx', 'chan')
- grad_filters: float32 [512, 128], P('chan')
All inputs are finite; a program needn't handle non-finite values.
Results may differ from a plain program's by a relative error of at most 0.0058.
Values may be sent and summed in bfloat16 or wider, within the bound.
A program may use at most 128 MiB of HBM per device.

v0:
```python
import jax
import jax.numpy as jnp
from jax import lax
from jax.sharding import PartitionSpec as P

D = 8192


def shifted(block, axis, distance):
    devices = range(lax.axis_size(axis))
    route = [(i - distance, i) for i in devices if i - distance in devices]
    return lax.ppermute(block, axis, route)


def toeplitz(taps):
    count, width = taps.shape
    zeros = jnp.zeros((count, width), taps.dtype)
    line = jnp.concatenate([zeros, jnp.flip(taps, 1), zeros], axis=1)
    tiled = jnp.tile(line, (1, width))
    tiled = tiled[:, : width * (3 * width - 1)].reshape(count, width, 3 * width - 1)
    return tiled[:, :, width - 1 : 3 * width - 1]


def lag_sums(pairs):
    count, width, double = pairs.shape
    flat = pairs.reshape(count, width * double)
    flat = jnp.concatenate([flat, jnp.zeros((count, width), pairs.dtype)], axis=1)
    skewed = flat.reshape(count, width, double + 1)
    totals = jnp.sum(skewed, axis=1)
    return jnp.flip(totals[:, 1 : width + 1], axis=1)


def channel_major(array, groups):
    batch, length, width = array.shape
    members = width // groups
    moved = array.reshape(batch, length, groups, members).transpose(2, 0, 3, 1)
    return moved.reshape(groups, batch * members, length)


def token_major(array, batch):
    groups, packed, length = array.shape
    members = packed // batch
    moved = array.reshape(groups, batch, members, length).transpose(1, 3, 0, 2)
    return moved.reshape(batch, length, groups * members)


def channel_sum(array, batch):
    groups, packed, length = array.shape
    members = packed // batch
    return jnp.sum(array.reshape(groups, batch, members, length), axis=(0, 2))


def spread(values, groups, members):
    batch, length = values.shape
    wide = jnp.broadcast_to(values[None, :, None, :], (groups, batch, members, length))
    return wide.reshape(groups, batch * members, length)


def body(query, key_in, value_in, cotangent, filters, norm_gain):
    batch, rows, width = query.shape
    groups, taps = filters.shape
    members = width // groups
    packed = batch * members
    blocks_n = rows // taps
    weights = toeplitz(filters.astype(jnp.bfloat16))
    query_cm = channel_major(query, groups)
    key_cm = channel_major(key_in, groups)
    value_cm = channel_major(value_in, groups)
    cotangent_cm = channel_major(cotangent, groups)
    signal = (key_cm.astype(jnp.float32) * value_cm.astype(jnp.float32)).astype(jnp.bfloat16)
    carried = shifted(signal, "ctx", 1)
    extent = signal.shape[2] // taps
    blocks = signal.reshape(groups, packed, extent, taps)
    before = jnp.concatenate([carried.reshape(groups, packed, 1, taps), blocks[:, :, :-1]], axis=2)
    window = jnp.concatenate([before, blocks], axis=3)
    mixed = jnp.einsum("gpks,gts->gpkt", window, weights, preferred_element_type=jnp.float32)
    mixed = mixed.reshape(groups, packed, extent * taps)
    gain_cm = norm_gain.reshape(groups, 1, members, 1).reshape(groups, packed, 1)
    lifted = query_cm.astype(jnp.float32) * mixed
    scaled = gain_cm * cotangent_cm.astype(jnp.float32)
    power, inner = lax.psum(
        (channel_sum(lifted * lifted, batch), channel_sum(scaled * lifted, batch)), "chan"
    )
    recip = spread(lax.rsqrt(power / D + 1e-06), groups, members)
    inner = spread(inner, groups, members)
    grad_mix = recip * scaled - lifted * recip**3 * inner / D
    grad_conv = (grad_mix * query_cm.astype(jnp.float32)).astype(jnp.bfloat16)
    later = shifted(grad_conv, "ctx", -1)
    normed = token_major((lifted * recip * gain_cm).astype(jnp.bfloat16), batch)
    grad_query = token_major((grad_mix * mixed).astype(jnp.bfloat16), batch)
    gathered = jnp.concatenate([grad_conv, later], axis=2).reshape(
        groups, packed, blocks_n + 1, taps
    )
    back = jnp.einsum("gpkt,gts->gpks", gathered, weights, preferred_element_type=jnp.float32)
    grad_signal = (back[:, :, :blocks_n, taps:] + back[:, :, 1:, :taps]).reshape(
        groups, packed, rows
    )
    grad_key = token_major((grad_signal * value_cm.astype(jnp.float32)).astype(jnp.bfloat16), batch)
    grad_value = token_major((grad_signal * key_cm.astype(jnp.float32)).astype(jnp.bfloat16), batch)
    own_blocks = grad_conv.reshape(groups, packed, blocks_n, taps)
    pairs = jnp.einsum("gpkt,gpks->gts", own_blocks, window, preferred_element_type=jnp.float32)
    grad_filters = lax.psum(lag_sums(pairs), "ctx")
    return (normed, grad_query, grad_key, grad_value, grad_filters)


def solution(mesh):
    placed = (
        P(None, "ctx", "chan"),
        P(None, "ctx", "chan"),
        P(None, "ctx", "chan"),
        P(None, "ctx", "chan"),
        P("chan", None),
        P("chan"),
    )
    return jax.shard_map(
        body,
        mesh=mesh,
        in_specs=placed,
        out_specs=(
            P(None, "ctx", "chan"),
            P(None, "ctx", "chan"),
            P(None, "ctx", "chan"),
            P(None, "ctx", "chan"),
            P("chan", None),
        ),
        check_vma=False,
    )
```

profile of v0, /device:TPU:0, one launch (start us, length us, event | category | flops | bytes accessed | tf_op | source)
XLA Modules:
  0.0 246.5 jit_solution(9024611935956841571)
XLA Ops:
  7.2 0.0 all-reduce.4.cloned.1.call-start
  7.2 1.3 multiply_convert_fusion.5
  8.5 0.3 copy.33
  8.8 4.9 %collective-permute-start = (bf16[128,16,128]{2,1,0:T(8,128)(2,1)S(1)}, bf16[128,16,128]{2,1,0:T(8,128)(2,1)S(1)}, u32[]{:S(2)}, u32[]{:S(2)}) collective-permute-start(bf16[128,16,128]{2,1,0:T(8,128)(2,1)S(1)} %bitcast.82), channel_id=1, source_target_pairs={{0,4},{4,8},{8,12},{12,16},{16,20},{20,24},{24,28},{1,5},{5,9},{9,... | collective-permute-start | bytes 1572872 | tf_op jit(solution)/shard_map/ppermute | solution.py:12
  13.7 0.8 convert_element_type.124
  14.6 0.1 rev.8
  14.7 0.8 mul.74
  15.5 1.2 copy.32
  16.7 1.2 copy.34
  18.0 5.7 %tile.4 = bf16[128,128,384]{2,1,0:T(8,128)(2,1)} broadcast(bf16[128,384]{1,0:T(8,128)(2,1)S(1)} %pad_maximum_fusion), dimensions={0,2} | broadcast | bytes 12681216 | tf_op jit(solution)/shard_map/tile | solution.py:19
  23.7 12.5 %copy.47 = bf16[16,8,128,384]{3,1,2,0:T(8,128)(2,1)S(1)} copy(bf16[16,8,128,384]{3,2,1,0:T(8,128)(2,1)} %bitcast.76) | data formatting | bytes 25165824
  36.1 5.2 %slice.20 = bf16[128,49024]{1,0:T(8,128)(2,1)} slice(bf16[128,49152]{1,0:T(8,128)(2,1)S(1)} %bitcast.77), slice={[0:128], [0:49024]} | slice | bytes 25100288 | tf_op jit(solution)/shard_map/slice | solution.py:20
  41.3 30.9 %reshape.148 = bf16[128,128,383]{2,1,0:T(8,128)(2,1)} reshape(bf16[128,49024]{1,0:T(8,128)(2,1)} %slice.20) | data formatting | bytes 25100288 | tf_op jit(solution)/shard_map/reshape | solution.py:20
  72.2 0.0 collective-permute-done
  72.2 0.0 copy-start.2
  72.2 9.0 %multiply_reduce_fusion = (f32[128]{0:T(128)S(1)}, f32[128]{0:T(128)S(1)}, f32[128,16,128]{2,1,0:T(8,128)}, f32[128,16,128]{2,1,0:T(8,128)}) fusion(f32[128,16,128]{2,1,0:T(8,128)S(1)} %bitcast.80, f32[128,16]{1,0:T(8,128)S(1)} %mul.74, f32[128,16,128]{2,1,0:T(8,128)S(1)} %bitcast.78, bf16[128,128,383]{2,1,0:T(8,128)(2,1)} %reshape.148, ...), kind=kOutput, calls=%fused_computation.16 | convolution fusion | flops 137887488 | bytes 13640704 | tf_op jit(solution)/shard_map/gpks,gts->gpkt/dot_general | solution.py:76
  81.2 6.3 %all-reduce.1 = (f32[1,128]{1,0:T(1,128)S(1)}, f32[128]{0:T(128)S(1)}) all-reduce(f32[1,128]{1,0:T(1,128)S(1)} %bitcast.93, f32[128]{0:T(128)S(1)} %get-tuple-element.20), channel_id=1, replica_groups=mesh['ctx'=8,'chan'=4] {'chan'}, use_global_device_ids=true, to_apply=%region_1.2 | all-reduce | flops 256 | bytes 2048 | tf_op jit(solution)/shard_map/psum | solution.py:81
  87.5 0.0 copy-done.2
  87.5 3.0 %multiply_convert_fusion.2 = (bf16[128,16,128]{2,1,0:T(8,128)(2,1)S(1)}, bf16[128,16,128]{2,1,0:T(8,128)(2,1)}, bf16[128,16,128]{2,1,0:T(8,128)(2,1)}) fusion(f32[128,16,128]{2,1,0:T(8,128)S(1)} %bitcast.79, f32[128]{0:T(128)S(1)} %get-tuple-element.23, f32[128,16,128]{2,1,0:T(8,128)} %get-tuple-element.24, f32[128]{0:T(128)S(1)} %multiply_multiply_fusion, ...), kind=kLoop, calls=%fused_computation.13 | loop fusion | flops 3407872 | bytes 5776896 | tf_op jit(solution)/shard_map/convert_element_type | solution.py:87
  90.5 1.5 collective-permute-start.1
  92.0 9.1 %fusion.8 = f32[128,128,256]{2,1,0:T(8,128)} fusion(bf16[128,16,128]{2,1,0:T(8,128)(2,1)S(1)} %get-tuple-element.27, bf16[128,16,1,128]{3,1,0,2:T(8,128)(2,1)S(1)} %bitcast.84, bf16[128,16,1,128]{3,1,0,2:T(8,128)(2,1)} %bitcast.88), kind=kOutput, calls=%fused_computation.20 | convolution fusion | flops 136314880 | bytes 18350080 | tf_op jit(solution)/shard_map/gpkt,gpks->gts/dot_general | solution.py:101
  101.1 17.8 %copy.45 = f32[128,128,256]{0,2,1:T(8,128)} copy(f32[128,128,256]{2,1,0:T(8,128)} %fusion.8) | data formatting | bytes 33554432 | tf_op jit(solution)/shard_map/reshape | solution.py:26
  118.9 13.3 %concatenate.15 = f32[128,32896]{0,1:T(8,128)} pad(f32[128,32768]{0,1:T(8,128)} %bitcast.75, f32[]{:T(128)} %constant.5.clone.1), padding=0_0x0_128 | pad | bytes 33619972 | tf_op jit(solution)/shard_map/concatenate | solution.py:27
  132.2 17.5 %reshape.161 = f32[128,128,257]{0,2,1:T(8,128)} reshape(f32[128,32896]{0,1:T(8,128)} %concatenate.15) | data formatting | bytes 33685504 | tf_op jit(solution)/shard_map/reshape | solution.py:28
  149.7 0.0 copy-start
  149.7 0.0 copy-start.1
  149.7 6.8 %reduce_sum.35 = f32[128,257]{0,1:T(8,128)S(1)} reduce(f32[128,128,257]{0,2,1:T(8,128)} %reshape.161, f32[]{:T(128)} %constant.5.clone.1), dimensions={1}, to_apply=%region_4.5 | reduce | flops 4177792 | bytes 16974340 | tf_op jit(solution)/shard_map/reduce_sum | solution.py:29
  156.5 0.6 rev.9
  157.2 0.0 all-reduce.4.cloned.1.call-update
  157.2 0.0 copy-done
  157.2 0.2 copy.37
  157.4 0.0 copy-done.1
  157.4 0.2 copy.36
  157.6 2.0 copy.40
  159.7 2.0 copy.39
  161.7 66.6 %all-reduce.4.cloned.1.call-done = f32[128,128]{0,1:T(8,128)} async-done(((f32[128,128]{0,1:T(8,128)}), f32[128,128]{0,1:T(8,128)}) %all-reduce.4.cloned.1.call-update) | async-done | bytes 65552 | tf_op jit(solution)/shard_map/psum | solution.py:102
  228.3 1.6 copy.43
  229.9 0.0 collective-permute-done.1
  229.9 7.4 %fusion = f32[128,16,2,256]{3,1,2,0:T(8,128)S(1)} fusion(bf16[128,128,383]{2,1,0:T(8,128)(2,1)} %reshape.148, bf16[128,16,128]{2,1,0:T(8,128)(2,1)} %collective-permute-done.1, bf16[128,16,128]{2,1,0:T(8,128)(2,1)S(1)} %get-tuple-element.27), kind=kOutput, calls=%fused_computation | convolution fusion | flops 270532608 | bytes 13631488 | tf_op jit(solution)/shard_map/gpkt,gts->gpks/dot_general | solution.py:94
  237.3 0.3 multiply_convert_fusion
  237.6 1.0 copy.42
  238.6 1.0 copy.41
  (5 shorter events, 0.0 us)
Async XLA Ops:
  7.2 221.2 %all-reduce.4.cloned.1.call-start = ((), (), s32[]{:S(2)}) async-start(), calls=%async_computation | async-start | bytes 131072 | tf_op jit(solution)/shard_map/psum | solution.py:102
  8.8 63.4 %collective-permute-start = (bf16[128,16,128]{2,1,0:T(8,128)(2,1)S(1)}, bf16[128,16,128]{2,1,0:T(8,128)(2,1)S(1)}, u32[]{:S(2)}, u32[]{:S(2)}) collective-permute-start(bf16[128,16,128]{2,1,0:T(8,128)(2,1)S(1)} %bitcast.82), channel_id=1, source_target_pairs={{0,4},{4,8},{8,12},{12,16},{16,20},{20,24},{24,28},{1,5},{5,9},{9,... | collective-permute-start | bytes 1572872 | tf_op jit(solution)/shard_map/ppermute | solution.py:12
  72.2 15.2 %copy-start.2 = (bf16[128,16,128]{2,1,0:T(8,128)(2,1)}, bf16[128,16,128]{2,1,0:T(8,128)(2,1)S(1)}, u32[]{:S(2)}) copy-start(bf16[128,16,128]{2,1,0:T(8,128)(2,1)S(1)} %collective-permute-done) | copy-start | bytes 1572868
  90.5 139.4 %collective-permute-start.1 = (bf16[128,16,128]{2,1,0:T(8,128)(2,1)S(1)}, bf16[128,16,128]{2,1,0:T(8,128)(2,1)}, u32[]{:S(2)}, u32[]{:S(2)}) collective-permute-start(bf16[128,16,128]{2,1,0:T(8,128)(2,1)S(1)} %get-tuple-element.27), channel_id=1, source_target_pairs={{4,0},{8,4},{12,8},{16,12},{20,16},{24,20},{28,24},{5,1},{9,5},{13... | collective-permute-start | bytes 1572872 | tf_op jit(solution)/shard_map/ppermute | solution.py:12
  149.7 7.5 %copy-start = (bf16[1,128,2048]{2,1,0:T(8,128)(2,1)S(1)}, bf16[1,128,2048]{2,1,0:T(8,128)(2,1)}, u32[]{:S(2)}) copy-start(bf16[1,128,2048]{2,1,0:T(8,128)(2,1)} %param.7) | copy-start | bytes 1572868
  149.7 7.7 %copy-start.1 = (bf16[1,128,2048]{2,1,0:T(8,128)(2,1)S(1)}, bf16[1,128,2048]{2,1,0:T(8,128)(2,1)}, u32[]{:S(2)}) copy-start(bf16[1,128,2048]{2,1,0:T(8,128)(2,1)} %param.8) | copy-start | bytes 1572868
Sparse Core Ops, SparseCore 0:
  157.3 70.9 all-reduce.3
where the time goes:
time: 248 us; the launch traced here: 246 us
  local copies, waits for them, and re-layouts  115 us (46%)
  waiting for transfers between devices  66.7 us (27%)
  matrix products  25.5 us (10%)
  between operations  14.1 us (6%)
  other arithmetic  12.4 us (5%)
  starting transfers between devices  6.4 us (3%)
  blocking collectives  6.27 us (3%)
    psum x1, waiting for transfers between devices, body(): grad_filters = lax.psum(lag_sums(pairs), 'ctx')  66.6 us
    reshape x1, local copies, waits for them, and re-layouts, toeplitz(): tiled[:, :width * (3 * width - 1)].reshape(count, width, 3 * width - 1)  30.9 us
    unnamed x12, local copies, waits for them, and re-layouts  20.2 us
    reshape x1, local copies, waits for them, and re-layouts, lag_sums(): flat = pairs.reshape(count, width * double)  17.8 us
    reshape x1, local copies, waits for them, and re-layouts, lag_sums(): skewed = flat.reshape(count, width, double + 1)  17.5 us
    concatenate x1, local copies, waits for them, and re-layouts, lag_sums(): jnp.concatenate([flat, jnp.zeros((count, width), pairs.dtype)], axis=1)  13.3 us
    dot_general x1, matrix products, body(): jnp.einsum('gpkt,gpks->gts', own_blocks, window, preferred_element_type=j...  9.13 us
    dot_general x1, matrix products, body(): jnp.einsum('gpks,gts->gpkt', window, weights, preferred_element_type=jnp....  8.96 us
  transfers between devices with their start and end apart: 3, of which 1 were waited for; matrix products, arithmetic and copies ran while one was open for 53% of the time, Pallas kernels for 0%

commit v1 on v0

v1 whole, which is shorter than its diff:
```python
import functools

import jax
import jax.numpy as jnp
from jax import lax
from jax.experimental import pallas as pl
from jax.experimental.pallas import tpu as pltpu
from jax.sharding import PartitionSpec as P

D = 8192
LANES = 256
MESH = pl.DeviceIdType.MESH


def iota(shape, axis):
    return lax.broadcasted_iota(jnp.int32, shape, axis)


def kernel(
    n_ctx, n_chan, members, own_sum,
    q_ref, k_ref, v_ref, ct_ref, f_ref, gain_ref,
    normed_ref, gq_ref, gk_ref, gv_ref, gf_ref,
    win, gwin, srev, fwd, bwd, frev, taps32, mixed, power, inner, stats, part, land,
    sig_send, sig_recv, gc_send, gc_recv, st_send, st_recv, rs_send, rs_recv, ag_send, ag_recv,
):
    f32, bf16 = jnp.float32, jnp.bfloat16
    rows = q_ref.shape[0]
    nb = q_ref.shape[1] // LANES
    groups = f_ref.shape[0]
    per = LANES // members
    me, chan = lax.axis_index("ctx"), lax.axis_index("chan")
    last = n_ctx - 1

    barrier = pltpu.get_barrier_semaphore()
    chan_peers = [lax.rem(chan + d, n_chan) for d in range(1, n_chan)]
    for peer in chan_peers:
        pl.semaphore_signal(barrier, inc=1, device_id=(me, peer), device_id_type=MESH)
    if own_sum:
        ctx_peers = [lax.rem(me + d, n_ctx) for d in range(1, n_ctx)]
        for peer in ctx_peers:
            pl.semaphore_signal(barrier, inc=1, device_id=(peer, chan), device_id_type=MESH)
        pl.semaphore_wait(barrier, n_chan - 1 + n_ctx - 1)
    else:
        for step in (1, n_ctx - 1):
            pl.semaphore_signal(
                barrier, inc=1, device_id=(lax.rem(me + step, n_ctx), chan), device_id_type=MESH
            )
        pl.semaphore_wait(barrier, n_chan - 1 + 2)

    def lanes(c):
        return pl.ds(pl.multiple_of(c * LANES, LANES), LANES)

    def signal_copy(c):
        return pltpu.make_async_remote_copy(
            src_ref=win.at[c, pl.ds(rows, rows), :],
            dst_ref=win.at[c, pl.ds(0, rows), :],
            send_sem=sig_send.at[c], recv_sem=sig_recv.at[c],
            device_id=(jnp.minimum(me + 1, last), chan), device_id_type=MESH,
        )

    def conv_copy(c):
        return pltpu.make_async_remote_copy(
            src_ref=gwin.at[c, pl.ds(0, rows), :],
            dst_ref=gwin.at[c, pl.ds(rows, rows), :],
            send_sem=gc_send.at[c], recv_sem=gc_recv.at[c],
            device_id=(jnp.maximum(me - 1, 0), chan), device_id_type=MESH,
        )

    @pl.loop(0, nb)
    def _(c):
        key = k_ref[:, lanes(c)].astype(f32)
        win[c, rows:, :] = (key * v_ref[:, lanes(c)].astype(f32)).astype(bf16)

        @pl.when(me < last)
        def _():
            signal_copy(c).start()

        @pl.when(me == 0)
        def _():
            win[c, :rows, :] = jnp.zeros((rows, LANES), bf16)

        @pl.when(me == last)
        def _():
            gwin[c, rows:, :] = jnp.zeros((rows, LANES), bf16)

    row, col = iota((rows, rows), 0), iota((rows, rows), 1)
    taps_b = f_ref[...].astype(bf16)
    taps32[...] = taps_b.astype(f32)
    negate = (lax.rem(row + col, rows) == 0).astype(f32).astype(bf16)
    frev[...] = jnp.dot(taps_b, negate, preferred_element_type=f32)

    @pl.loop(0, groups)
    def _(g):
        at = pl.ds(pl.multiple_of(g * rows, rows), rows)
        turned = jnp.broadcast_to(frev[pl.ds(g, 1), :], (rows, rows))
        turned = pltpu.roll(turned, 0, 1, stride=1, stride_axis=0)
        fwd[at, :rows] = jnp.where(col > row, turned, 0.0).astype(bf16)
        fwd[at, rows:] = jnp.where(col <= row, turned, 0.0).astype(bf16)
        plain = jnp.broadcast_to(taps32[pl.ds(g, 1), :], (rows, rows))
        plain = pltpu.roll(plain, 0, 1, stride=1, stride_axis=0)
        bwd[at, :rows] = jnp.where(col >= row, plain, 0.0).astype(bf16)
        bwd[at, rows:] = jnp.where(col < row, plain, 0.0).astype(bf16)

    lane_group = iota((rows, LANES), 1) // members
    flip = (row + col == rows - 1).astype(f32).astype(bf16)
    power[...] = jnp.zeros_like(power)
    inner[...] = jnp.zeros_like(inner)

    def filtered(matrices, window, c):
        total = jnp.zeros((rows, LANES), f32)
        for k in range(per):
            at = pl.ds(pl.multiple_of((c * per + k) * rows, rows), rows)
            out = jnp.dot(matrices[at, :], window, preferred_element_type=f32)
            total = jnp.where(lane_group == k, out, total)
        return total

    @pl.loop(0, nb)
    def _(c):
        @pl.when(me > 0)
        def _():
            signal_copy(c).wait_recv()

        window = win[c]
        mix = filtered(fwd, window, c)
        mixed[c] = mix
        lifted = q_ref[:, lanes(c)].astype(f32) * mix
        scaled = gain_ref[:, lanes(c)] * ct_ref[:, lanes(c)].astype(f32)
        square, cross = lifted * lifted, scaled * lifted
        half = LANES // 2
        power[...] += square[:, :half] + square[:, half:]
        inner[...] += cross[:, :half] + cross[:, half:]
        srev[c, :rows, :] = jnp.dot(flip, window[rows:], preferred_element_type=f32).astype(bf16)
        srev[c, rows:, :] = jnp.dot(flip, window[:rows], preferred_element_type=f32).astype(bf16)

    stats[chan, 0:1, :] = jnp.sum(power[...].T, axis=0, keepdims=True)
    stats[chan, 1:2, :] = jnp.sum(inner[...].T, axis=0, keepdims=True)
    stats[chan, 2:, :] = jnp.zeros((6, rows), f32)

    def stat_copy(d, slot):
        return pltpu.make_async_remote_copy(
            src_ref=stats.at[slot], dst_ref=stats.at[slot],
            send_sem=st_send.at[d], recv_sem=st_recv.at[d],
            device_id=(me, chan_peers[d]), device_id_type=MESH,
        )

    for d in range(n_chan - 1):
        stat_copy(d, chan).start()
    for d in range(n_chan - 1):
        stat_copy(d, lax.rem(chan + n_chan - d - 1, n_chan)).wait_recv()
    sums = jnp.sum(stats[...], axis=0)
    recip_row = lax.rsqrt(sums[0:1] / D + 1e-06)
    slope_row = recip_row * recip_row * recip_row * sums[1:2] / D
    recip = jnp.broadcast_to(recip_row, (rows, rows)).T
    slope = jnp.broadcast_to(slope_row, (rows, rows)).T
    power[...] = recip
    inner[...] = slope

    @pl.loop(0, nb)
    def _(c):
        recip = jnp.concatenate([power[...]] * (LANES // rows), axis=1)
        slope = jnp.concatenate([inner[...]] * (LANES // rows), axis=1)
        mix = mixed[c]
        query = q_ref[:, lanes(c)].astype(f32)
        gain = gain_ref[:, lanes(c)]
        lifted = query * mix
        scaled = gain * ct_ref[:, lanes(c)].astype(f32)
        grad_mix = recip * scaled - lifted * slope
        gwin[c, :rows, :] = (grad_mix * query).astype(bf16)

        @pl.when(me > 0)
        def _():
            conv_copy(c).start()

        normed_ref[:, lanes(c)] = (lifted * recip * gain).astype(bf16)
        gq_ref[:, lanes(c)] = (grad_mix * mix).astype(bf16)

    @pl.loop(0, nb)
    def _(c):
        conv = gwin[c, :rows, :].astype(f32)
        turned = srev[c]
        for k in range(per):
            masked = jnp.where(lane_group == k, conv, 0.0).astype(bf16)
            pairs = lax.dot_general(
                masked, turned, (((1,), (1,)), ((), ())), preferred_element_type=f32
            )
            both = jnp.where(row + col >= rows - 1, pairs[:, :rows], pairs[:, rows:])
            both = pltpu.roll(both, 1, 1, stride=1, stride_axis=0)
            part[pl.ds(c * per + k, 1), :] = jnp.sum(both, axis=0, keepdims=True)

    share = groups // n_ctx

    def scatter_copy(d):
        peer = ctx_peers[d]
        return pltpu.make_async_remote_copy(
            src_ref=part.at[pl.ds(pl.multiple_of(peer * share, share), share), :],
            dst_ref=land.at[d],
            send_sem=rs_send.at[d], recv_sem=rs_recv.at[d],
            device_id=(peer, chan), device_id_type=MESH,
        )

    def gather_copy(d, owner):
        at = pl.ds(pl.multiple_of(owner * share, share), share)
        return pltpu.make_async_remote_copy(
            src_ref=gf_ref.at[at, :], dst_ref=gf_ref.at[at, :],
            send_sem=ag_send.at[d], recv_sem=ag_recv.at[d],
            device_id=(ctx_peers[d], chan), device_id_type=MESH,
        )

    if own_sum:
        for d in range(n_ctx - 1):
            scatter_copy(d).start()
    else:
        gf_ref[...] = part[...]

    def back(c):
        @pl.when(me < last)
        def _():
            conv_copy(c).wait_recv()

        grad_signal = filtered(bwd, gwin[c], c)
        gk_ref[:, lanes(c)] = (grad_signal * v_ref[:, lanes(c)].astype(f32)).astype(bf16)
        gv_ref[:, lanes(c)] = (grad_signal * k_ref[:, lanes(c)].astype(f32)).astype(bf16)

    pl.loop(0, nb // 2)(back)
    if own_sum:
        for d in range(n_ctx - 1):
            scatter_copy(d).wait_recv()
        at = pl.ds(pl.multiple_of(me * share, share), share)
        gf_ref[at, :] = part[at, :] + jnp.sum(land[...], axis=0)
        for d in range(n_ctx - 1):
            gather_copy(d, me).start()
    pl.loop(nb // 2, nb)(back)

    if own_sum:
        for d in range(n_ctx - 1):
            gather_copy(d, lax.rem(me + n_ctx - d - 1, n_ctx)).wait_recv()
            gather_copy(d, me).wait_send()
            scatter_copy(d).wait_send()
    for d in range(n_chan - 1):
        stat_copy(d, chan).wait_send()

    @pl.loop(0, nb)
    def _(c):
        @pl.when(me < last)
        def _():
            signal_copy(c).wait_send()

        @pl.when(me > 0)
        def _():
            conv_copy(c).wait_send()


def body(n_ctx, n_chan, query, key_in, value_in, cotangent, filters, norm_gain):
    batch, rows, width = query.shape
    groups, taps = filters.shape
    assert batch == 1 and rows == taps
    members = width // groups
    nb = width // LANES
    own_sum = groups % (8 * n_ctx) == 0
    share = max(groups // n_ctx, 8)
    f32, bf16 = jnp.float32, jnp.bfloat16
    flat = jax.ShapeDtypeStruct((rows, width), bf16)
    vmem = pl.BlockSpec(memory_space=pltpu.VMEM)
    dma = pltpu.SemaphoreType.DMA
    outs = pl.pallas_call(
        functools.partial(kernel, n_ctx, n_chan, members, own_sum),
        out_shape=(flat, flat, flat, flat, jax.ShapeDtypeStruct((groups, taps), f32)),
        in_specs=[vmem] * 6,
        out_specs=(vmem,) * 5,
        scratch_shapes=[
            pltpu.VMEM((nb, 2 * rows, LANES), bf16),
            pltpu.VMEM((nb, 2 * rows, LANES), bf16),
            pltpu.VMEM((nb, 2 * rows, LANES), bf16),
            pltpu.VMEM((groups * rows, 2 * rows), bf16),
            pltpu.VMEM((groups * rows, 2 * rows), bf16),
            pltpu.VMEM((groups, taps), f32),
            pltpu.VMEM((groups, taps), f32),
            pltpu.VMEM((nb, rows, LANES), f32),
            pltpu.VMEM((rows, rows), f32),
            pltpu.VMEM((rows, rows), f32),
            pltpu.VMEM((n_chan, 8, rows), f32),
            pltpu.VMEM((groups, taps), f32),
            pltpu.VMEM((n_ctx - 1, share, taps), f32),
            dma((nb,)), dma((nb,)), dma((nb,)), dma((nb,)),
            dma((n_chan - 1,)), dma((n_chan - 1,)),
            dma((n_ctx - 1,)), dma((n_ctx - 1,)), dma((n_ctx - 1,)), dma((n_ctx - 1,)),
        ],
        compiler_params=pltpu.CompilerParams(
            collective_id=0, has_side_effects=True, vmem_limit_bytes=48 << 20
        ),
    )(
        *(x.reshape(rows, width) for x in (query, key_in, value_in, cotangent)),
        filters,
        norm_gain.reshape(1, width),
    )
    grad_filters = outs[4] if own_sum else lax.psum(outs[4], "ctx")
    return tuple(x.reshape(1, rows, width) for x in outs[:4]) + (grad_filters,)


def solution(mesh):
    spread = P(None, "ctx", "chan")
    return jax.shard_map(
        functools.partial(body, mesh.shape["ctx"], mesh.shape["chan"]),
        mesh=mesh,
        in_specs=(spread,) * 4 + (P("chan", None), P("chan")),
        out_specs=(spread,) * 4 + (P("chan", None),),
        check_vma=False,
    )
```

time: 248 us -> 55.8 us (0.22)
  local copies, waits for them, and re-layouts: 115 us -> 9.5 us
  waiting for transfers between devices: 66.7 us -> 0 us
  Pallas kernels: 0 us -> 45.3 us
  matrix products: 25.5 us -> 0 us
  between operations: 14.1 us -> 0.66 us
  other arithmetic: 12.4 us -> 0 us
  starting transfers between devices: 6.4 us -> 0 us
  blocking collectives: 6.27 us -> 0 us
    psum x1 -> x0, waiting for transfers between devices: 66.6 us -> none  [body(): grad_filters = lax.psum(lag_sums(pairs), 'ctx')]
    reshape x3 -> x0, local copies, waits for them, and re-layouts: 66.1 us -> none  [the longest x1 30.9 us: toeplitz(): tiled[:, :width * (3 * width - 1)].reshape(count, width, 3 * width - 1)]
    pallas_call x0 -> x1, Pallas kernels: none -> 45.3 us  [body(): pl.pallas_call(functools.partial(kernel, n_ctx, n_chan, members, own_sum)...]
    dot_general x3 -> x0, matrix products: 25.5 us -> none  [the longest x1 9.13 us: body(): jnp.einsum('gpkt,gpks->gts', own_blocks, window, preferred_element_type=j...]
    concatenate x1 -> x0, local copies, waits for them, and re-layouts: 13.3 us -> none  [lag_sums(): jnp.concatenate([flat, jnp.zeros((count, width), pairs.dtype)], axis=1)]
    unnamed x12 -> x17, local copies, waits for them, and re-layouts: 20.2 us -> 9.5 us
    reduce_sum x1 -> x0, other arithmetic: 6.82 us -> none  [lag_sums(): totals = jnp.sum(skewed, axis=1)]
    ppermute x2 -> x0, starting transfers between devices: 6.36 us -> none  [shifted(): return lax.ppermute(block, axis, route)]
  transfers between devices with their start and end apart: 3 -> 0, of which waited for: 1 -> 0; matrix products, arithmetic and copies ran while one was open for 53% -> 0% of each run, Pallas kernels for 0% -> 0%
where the time goes in v1:
time: 55.8 us; the launch traced here: 55.4 us
  Pallas kernels  45.3 us (81%)
  local copies, waits for them, and re-layouts  9.5 us (17%)
  between operations  0.66 us (1%)
    pallas_call x1, Pallas kernels, body(): pl.pallas_call(functools.partial(kernel, n_ctx, n_chan, members, own_sum)...  45.3 us
    unnamed x17, local copies, waits for them, and re-layouts  9.5 us

profile of v1, /device:TPU:0, one launch (start us, length us, event | category | flops | bytes accessed | tf_op | source)
XLA Modules:
  0.0 55.4 jit_solution(15380371366115664289)
XLA Ops:
  0.6 0.0 copy-start.5
  0.6 0.7 %copy-done.5 = f32[2048]{0:T(1024)S(1)} copy-done((f32[2048]{0:T(1024)S(1)}, f32[2048]{0:T(1024)}, u32[]{:S(2)}) %copy-start.5) | copy-done | bytes 8216
  1.3 0.0 copy-start
  1.3 1.0 %copy-done = bf16[1,128,2048]{2,1,0:T(8,128)(2,1)S(1)} copy-done((bf16[1,128,2048]{2,1,0:T(8,128)(2,1)S(1)}, bf16[1,128,2048]{2,1,0:T(8,128)(2,1)}, u32[]{:S(2)}) %copy-start) | copy-done | bytes 524312
  2.4 0.0 copy-start.1
  2.4 1.0 %copy-done.1 = bf16[1,128,2048]{2,1,0:T(8,128)(2,1)S(1)} copy-done((bf16[1,128,2048]{2,1,0:T(8,128)(2,1)S(1)}, bf16[1,128,2048]{2,1,0:T(8,128)(2,1)}, u32[]{:S(2)}) %copy-start.1) | copy-done | bytes 524312
  3.4 0.0 copy-start.2
  3.4 1.0 %copy-done.2 = bf16[1,128,2048]{2,1,0:T(8,128)(2,1)S(1)} copy-done((bf16[1,128,2048]{2,1,0:T(8,128)(2,1)S(1)}, bf16[1,128,2048]{2,1,0:T(8,128)(2,1)}, u32[]{:S(2)}) %copy-start.2) | copy-done | bytes 524312
  4.5 0.0 copy-start.3
  4.5 1.0 %copy-done.3 = bf16[1,128,2048]{2,1,0:T(8,128)(2,1)S(1)} copy-done((bf16[1,128,2048]{2,1,0:T(8,128)(2,1)S(1)}, bf16[1,128,2048]{2,1,0:T(8,128)(2,1)}, u32[]{:S(2)}) %copy-start.3) | copy-done | bytes 524312
  5.5 0.0 copy-start.4
  5.5 0.8 %copy-done.4 = f32[128,128]{1,0:T(8,128)S(1)} copy-done((f32[128,128]{1,0:T(8,128)S(1)}, f32[128,128]{1,0:T(8,128)}, u32[]{:S(2)}) %copy-start.4) | copy-done | bytes 65560
  6.3 45.3 %shard_map.101 = (bf16[128,2048]{1,0:T(8,128)(2,1)S(1)}, bf16[128,2048]{1,0:T(8,128)(2,1)S(1)}, bf16[128,2048]{1,0:T(8,128)(2,1)S(1)}, bf16[128,2048]{1,0:T(8,128)(2,1)S(1)}, f32[128,128]{1,0:T(8,128)S(1)}) custom-call(bf16[128,2048]{1,0:T(8,128)(2,1)S(1)} %bitcast.13, bf16[128,2048]{1,0:T(8,128)(2,1)S(1)} %bitcast.14, bf16[128,2048]{1,0:T(8,128)(2,1)S(1)} %bitcast.15, ...), custom_call_target="tpu_custom_call" | custom-call | tf_op jit(solution)/shard_map/pallas_call | solution.py:265
  51.6 0.8 %copy.16 = bf16[1,128,2048]{2,1,0:T(8,128)(2,1)} copy(bf16[1,128,2048]{2,1,0:T(8,128)(2,1)S(1)} %bitcast.12) | data formatting | bytes 1048576
  52.4 0.8 %copy.17 = bf16[1,128,2048]{2,1,0:T(8,128)(2,1)} copy(bf16[1,128,2048]{2,1,0:T(8,128)(2,1)S(1)} %bitcast.11) | data formatting | bytes 1048576
  53.2 0.8 %copy.18 = bf16[1,128,2048]{2,1,0:T(8,128)(2,1)} copy(bf16[1,128,2048]{2,1,0:T(8,128)(2,1)S(1)} %bitcast.10) | data formatting | bytes 1048576
  54.0 0.8 %copy.19 = bf16[1,128,2048]{2,1,0:T(8,128)(2,1)} copy(bf16[1,128,2048]{2,1,0:T(8,128)(2,1)S(1)} %bitcast.9) | data formatting | bytes 1048576
  54.8 0.6 %copy.20 = f32[128,128]{1,0:T(8,128)} copy(f32[128,128]{1,0:T(8,128)S(1)} %get-tuple-element.24) | data formatting | bytes 131072
Async XLA Ops:
  0.6 0.7 %copy-start.5 = (f32[2048]{0:T(1024)S(1)}, f32[2048]{0:T(1024)}, u32[]{:S(2)}) copy-start(f32[2048]{0:T(1024)} %param.11) | copy-start | bytes 24580
  1.3 1.0 %copy-start = (bf16[1,128,2048]{2,1,0:T(8,128)(2,1)S(1)}, bf16[1,128,2048]{2,1,0:T(8,128)(2,1)}, u32[]{:S(2)}) copy-start(bf16[1,128,2048]{2,1,0:T(8,128)(2,1)} %param.6) | copy-start | bytes 1572868
  2.4 1.0 %copy-start.1 = (bf16[1,128,2048]{2,1,0:T(8,128)(2,1)S(1)}, bf16[1,128,2048]{2,1,0:T(8,128)(2,1)}, u32[]{:S(2)}) copy-start(bf16[1,128,2048]{2,1,0:T(8,128)(2,1)} %param.7) | copy-start | bytes 1572868
  3.4 1.0 %copy-start.2 = (bf16[1,128,2048]{2,1,0:T(8,128)(2,1)S(1)}, bf16[1,128,2048]{2,1,0:T(8,128)(2,1)}, u32[]{:S(2)}) copy-start(bf16[1,128,2048]{2,1,0:T(8,128)(2,1)} %param.8) | copy-start | bytes 1572868
  4.5 1.0 %copy-start.3 = (bf16[1,128,2048]{2,1,0:T(8,128)(2,1)S(1)}, bf16[1,128,2048]{2,1,0:T(8,128)(2,1)}, u32[]{:S(2)}) copy-start(bf16[1,128,2048]{2,1,0:T(8,128)(2,1)} %param.9) | copy-start | bytes 1572868
  5.5 0.8 %copy-start.4 = (f32[128,128]{1,0:T(8,128)S(1)}, f32[128,128]{1,0:T(8,128)}, u32[]{:S(2)}) copy-start(f32[128,128]{1,0:T(8,128)} %f_ref.1) | copy-start | bytes 196612

commit v2 on v1

v2 whole, which is shorter than its diff:
```python
import functools

import jax
import jax.numpy as jnp
from jax import lax
from jax.experimental import pallas as pl
from jax.experimental.pallas import tpu as pltpu
from jax.sharding import PartitionSpec as P

D = 8192
LANES = 256
MESH = pl.DeviceIdType.MESH


def iota(shape, axis):
    return lax.broadcasted_iota(jnp.int32, shape, axis)


def kernel(
    n_ctx, n_chan, members, own_sum,
    q_hbm, k_hbm, v_hbm, ct_hbm, f_hbm, gain_hbm,
    normed_hbm, gq_hbm, gk_hbm, gv_hbm, gf_hbm,
    normed_ref, gq_ref, gk_ref, gv_ref, gf_ref, out_sem, gk_sem, gv_sem,
    q_ref, k_ref, v_ref, ct_ref, f_ref, gain_ref, in_sem,
    win, gwin, srev, own, fwd, frev, mixed, power, inner, stats, part, land,
    sig_send, sig_recv, gc_send, gc_recv, st_send, st_recv, rs_send, rs_recv, ag_send, ag_recv,
):
    f32, bf16 = jnp.float32, jnp.bfloat16
    rows = q_ref.shape[0]
    nb = q_ref.shape[1] // LANES
    groups = f_ref.shape[0]
    per = LANES // members
    me, chan = lax.axis_index("ctx"), lax.axis_index("chan")
    last = n_ctx - 1

    loads = [
        pltpu.make_async_copy(src, dst, in_sem.at[n])
        for n, (src, dst) in enumerate([
            (k_hbm, k_ref), (v_hbm, v_ref), (f_hbm, f_ref),
            (q_hbm, q_ref), (ct_hbm, ct_ref), (gain_hbm, gain_ref),
        ])
    ]
    for load in loads:
        load.start()
    barrier = pltpu.get_barrier_semaphore()
    chan_peers = [lax.rem(chan + d, n_chan) for d in range(1, n_chan)]
    near = range(1, n_ctx) if own_sum else sorted({1, n_ctx - 1})
    for peer in chan_peers:
        pl.semaphore_signal(barrier, inc=1, device_id=(me, peer), device_id_type=MESH)
    for d in near:
        pl.semaphore_signal(
            barrier, inc=1, device_id=(lax.rem(me + d, n_ctx), chan), device_id_type=MESH
        )

    def ctx_peer(d):
        return lax.rem(me + d + 1, n_ctx)

    def lanes(c):
        return pl.ds(pl.multiple_of(c * LANES, LANES), LANES)

    def signal_copy(c):
        return pltpu.make_async_remote_copy(
            src_ref=win.at[c, pl.ds(rows, rows), :],
            dst_ref=win.at[c, pl.ds(0, rows), :],
            send_sem=sig_send.at[c], recv_sem=sig_recv.at[c],
            device_id=(jnp.minimum(me + 1, last), chan), device_id_type=MESH,
        )

    def conv_copy(c):
        return pltpu.make_async_remote_copy(
            src_ref=gwin.at[c, pl.ds(rows, rows), :],
            dst_ref=gwin.at[c, pl.ds(0, rows), :],
            send_sem=gc_send.at[c], recv_sem=gc_recv.at[c],
            device_id=(jnp.maximum(me - 1, 0), chan), device_id_type=MESH,
        )

    loads[0].wait()
    loads[1].wait()

    @pl.loop(0, nb)
    def _(c):
        key = k_ref[:, lanes(c)].astype(f32)
        win[c, rows:, :] = (key * v_ref[:, lanes(c)].astype(f32)).astype(bf16)

        @pl.when(me == 0)
        def _():
            win[c, :rows, :] = jnp.zeros((rows, LANES), bf16)

        @pl.when(me == last)
        def _():
            gwin[c, :rows, :] = jnp.zeros((rows, LANES), bf16)

    pl.semaphore_wait(barrier, n_chan - 1 + len(near))

    @pl.when(me < last)
    def _():
        @pl.loop(0, nb)
        def _(c):
            signal_copy(c).start()

    row, col = iota((rows, rows), 0), iota((rows, rows), 1)
    loads[2].wait()
    taps_b = f_ref[...].astype(bf16)
    negate = (lax.rem(row + col, rows) == 0).astype(f32).astype(bf16)
    frev[...] = jnp.dot(taps_b, negate, preferred_element_type=f32)

    @pl.loop(0, groups)
    def _(g):
        at = pl.ds(pl.multiple_of(g * rows, rows), rows)
        turned = jnp.broadcast_to(frev[pl.ds(g, 1), :], (rows, rows))
        turned = pltpu.roll(turned, 0, 1, stride=1, stride_axis=0)
        fwd[at, :rows] = jnp.where(col > row, turned, 0.0).astype(bf16)
        fwd[at, rows:] = jnp.where(col <= row, turned, 0.0).astype(bf16)

    lane_group = iota((rows, LANES), 1) // members
    flip = (row + col == rows - 1).astype(f32).astype(bf16)
    power[...] = jnp.zeros_like(power)
    inner[...] = jnp.zeros_like(inner)
    for load in loads[3:]:
        load.wait()

    def filtered(window, c):
        total = jnp.zeros((rows, LANES), f32)
        for k in range(per):
            at = pl.ds(pl.multiple_of((c * per + k) * rows, rows), rows)
            out = jnp.dot(fwd[at, :], window, preferred_element_type=f32)
            total = jnp.where(lane_group == k, out, total)
        return total

    @pl.loop(0, nb)
    def _(c):
        @pl.when(me > 0)
        def _():
            signal_copy(c).wait_recv()

        window = win[c]
        mix = filtered(window, c)
        mixed[c] = mix
        lifted = q_ref[:, lanes(c)].astype(f32) * mix
        scaled = gain_ref[:, lanes(c)] * ct_ref[:, lanes(c)].astype(f32)
        square, cross = lifted * lifted, scaled * lifted
        half = LANES // 2
        power[...] += square[:, :half] + square[:, half:]
        inner[...] += cross[:, :half] + cross[:, half:]
        srev[c, :rows, :] = jnp.dot(flip, window[rows:], preferred_element_type=f32).astype(bf16)
        srev[c, rows:, :] = jnp.dot(flip, window[:rows], preferred_element_type=f32).astype(bf16)

    stats[chan, 0:1, :] = jnp.sum(power[...].T, axis=0, keepdims=True)
    stats[chan, 1:2, :] = jnp.sum(inner[...].T, axis=0, keepdims=True)
    stats[chan, 2:, :] = jnp.zeros((6, rows), f32)

    def stat_copy(d, slot):
        return pltpu.make_async_remote_copy(
            src_ref=stats.at[slot], dst_ref=stats.at[slot],
            send_sem=st_send.at[d], recv_sem=st_recv.at[d],
            device_id=(me, chan_peers[d]), device_id_type=MESH,
        )

    for d in range(n_chan - 1):
        stat_copy(d, chan).start()
    for d in range(n_chan - 1):
        stat_copy(d, lax.rem(chan + n_chan - d - 1, n_chan)).wait_recv()
    sums = jnp.sum(stats[...], axis=0)
    recip_row = lax.rsqrt(sums[0:1] / D + 1e-06)
    slope_row = recip_row * recip_row * recip_row * sums[1:2] / D
    recip = jnp.broadcast_to(recip_row, (rows, rows)).T
    slope = jnp.broadcast_to(slope_row, (rows, rows)).T
    power[...] = recip
    inner[...] = slope

    @pl.loop(0, nb)
    def _(c):
        recip = jnp.concatenate([power[...]] * (LANES // rows), axis=1)
        slope = jnp.concatenate([inner[...]] * (LANES // rows), axis=1)
        mix = mixed[c]
        query = q_ref[:, lanes(c)].astype(f32)
        gain = gain_ref[:, lanes(c)]
        lifted = query * mix
        scaled = gain * ct_ref[:, lanes(c)].astype(f32)
        grad_mix = recip * scaled - lifted * slope
        conv = (grad_mix * query).astype(bf16)
        own[c] = conv
        gwin[c, rows:, :] = jnp.dot(flip, conv, preferred_element_type=f32).astype(bf16)

        @pl.when(me > 0)
        def _():
            conv_copy(c).start()

        normed_ref[:, lanes(c)] = (lifted * recip * gain).astype(bf16)
        gq_ref[:, lanes(c)] = (grad_mix * mix).astype(bf16)

    saves = [
        pltpu.make_async_copy(src, dst, out_sem.at[n])
        for n, (src, dst) in enumerate(
            [(normed_ref, normed_hbm), (gq_ref, gq_hbm), (gf_ref, gf_hbm)]
        )
    ]
    saves[0].start()
    saves[1].start()

    def key_save(c):
        return pltpu.make_async_copy(
            gk_ref.at[:, lanes(c)], gk_hbm.at[:, lanes(c)], gk_sem.at[c]
        )

    def value_save(c):
        return pltpu.make_async_copy(
            gv_ref.at[:, lanes(c)], gv_hbm.at[:, lanes(c)], gv_sem.at[c]
        )

    def scatter_copy(d):
        peer = ctx_peer(d)
        return pltpu.make_async_remote_copy(
            src_ref=part.at[pl.ds(pl.multiple_of(peer * per, per), per), :],
            dst_ref=land.at[d],
            send_sem=rs_send.at[d], recv_sem=rs_recv.at[d],
            device_id=(peer, chan), device_id_type=MESH,
        )

    def gather_copy(d, owner):
        at = pl.ds(pl.multiple_of(owner * per, per), per)
        return pltpu.make_async_remote_copy(
            src_ref=gf_ref.at[at, :], dst_ref=gf_ref.at[at, :],
            send_sem=ag_send.at[d], recv_sem=ag_recv.at[d],
            device_id=(ctx_peer(d), chan), device_id_type=MESH,
        )

    @pl.loop(0, nb)
    def _(i):
        c = lax.rem(me + 1 + i, nb) if own_sum else i
        conv = own[c].astype(f32)
        turned = srev[c]
        for k in range(per):
            masked = jnp.where(lane_group == k, conv, 0.0).astype(bf16)
            pairs = lax.dot_general(
                masked, turned, (((1,), (1,)), ((), ())), preferred_element_type=f32
            )
            both = jnp.where(row + col >= rows - 1, pairs[:, :rows], pairs[:, rows:])
            both = pltpu.roll(both, 1, 1, stride=1, stride_axis=0)
            part[pl.ds(c * per + k, 1), :] = jnp.sum(both, axis=0, keepdims=True)
        if own_sum:
            @pl.when(i < nb - 1)
            def _():
                scatter_copy(i).start()

    def back(c):
        @pl.when(me < last)
        def _():
            conv_copy(c).wait_recv()

        turned = filtered(gwin[c], c)
        high = turned.astype(bf16)
        low = (turned - high.astype(f32)).astype(bf16)
        grad_signal = jnp.dot(
            jnp.concatenate([flip, flip], axis=1),
            jnp.concatenate([high, low], axis=0),
            preferred_element_type=f32,
        )
        gk_ref[:, lanes(c)] = (grad_signal * v_ref[:, lanes(c)].astype(f32)).astype(bf16)
        gv_ref[:, lanes(c)] = (grad_signal * k_ref[:, lanes(c)].astype(f32)).astype(bf16)
        key_save(c).start()
        value_save(c).start()

    pl.loop(0, nb // 2)(back)
    if own_sum:
        for d in range(n_ctx - 1):
            scatter_copy(d).wait_recv()
        at = pl.ds(pl.multiple_of(me * per, per), per)
        gf_ref[at, :] = part[at, :] + jnp.sum(land[...], axis=0)
        for d in range(n_ctx - 1):
            gather_copy(d, me).start()
    else:
        gf_ref[...] = part[...]
    pl.loop(nb // 2, nb)(back)

    if own_sum:
        for d in range(n_ctx - 1):
            gather_copy(d, lax.rem(me + n_ctx - d - 1, n_ctx)).wait_recv()
        saves[2].start()
        for d in range(n_ctx - 1):
            gather_copy(d, me).wait_send()
            scatter_copy(d).wait_send()
    else:
        saves[2].start()
    for d in range(n_chan - 1):
        stat_copy(d, chan).wait_send()

    @pl.loop(0, nb)
    def _(c):
        @pl.when(me < last)
        def _():
            signal_copy(c).wait_send()

        @pl.when(me > 0)
        def _():
            conv_copy(c).wait_send()

        key_save(c).wait()
        value_save(c).wait()

    for save in saves:
        save.wait()


def store(*refs):
    held, taken, given = refs[10:15], refs[15], refs[16]
    reads = [pltpu.make_async_copy(refs[n], held[n], taken.at[n]) for n in range(5)]
    writes = [pltpu.make_async_copy(held[n], refs[5 + n], given.at[n]) for n in range(5)]
    for copy in reads:
        copy.start()
    for read, write in zip(reads, writes):
        read.wait()
        write.start()
    for copy in writes:
        copy.wait()


def body(n_ctx, n_chan, query, key_in, value_in, cotangent, filters, norm_gain):
    batch, rows, width = query.shape
    groups, taps = filters.shape
    assert batch == 1 and rows == taps
    members = width // groups
    nb = width // LANES
    own_sum = nb == n_ctx
    f32, bf16 = jnp.float32, jnp.bfloat16
    flat = jax.ShapeDtypeStruct((rows, width), bf16)
    hbm = pl.BlockSpec(memory_space=pltpu.HBM)
    dma = pltpu.SemaphoreType.DMA
    outs = pl.pallas_call(
        functools.partial(kernel, n_ctx, n_chan, members, own_sum),
        out_shape=(flat, flat, flat, flat, jax.ShapeDtypeStruct((groups, taps), f32)),
        in_specs=[hbm] * 6,
        out_specs=(hbm,) * 5,
        scratch_shapes=[
            *[pltpu.VMEM((rows, width), bf16)] * 4,
            pltpu.VMEM((groups, taps), f32),
            dma((3,)), dma((nb,)), dma((nb,)),
            *[pltpu.VMEM((rows, width), bf16)] * 4,
            pltpu.VMEM((groups, taps), f32),
            pltpu.VMEM((1, width), f32),
            dma((6,)),
            pltpu.VMEM((nb, 2 * rows, LANES), bf16),
            pltpu.VMEM((nb, 2 * rows, LANES), bf16),
            pltpu.VMEM((nb, 2 * rows, LANES), bf16),
            pltpu.VMEM((nb, rows, LANES), bf16),
            pltpu.VMEM((groups * rows, 2 * rows), bf16),
            pltpu.VMEM((groups, taps), f32),
            pltpu.VMEM((nb, rows, LANES), f32),
            pltpu.VMEM((rows, rows), f32),
            pltpu.VMEM((rows, rows), f32),
            pltpu.VMEM((n_chan, 8, rows), f32),
            pltpu.VMEM((groups, taps), f32),
            pltpu.VMEM((n_ctx - 1, LANES // members, taps), f32),
            dma((nb,)), dma((nb,)), dma((nb,)), dma((nb,)),
            dma((n_chan - 1,)), dma((n_chan - 1,)),
            dma((n_ctx - 1,)), dma((n_ctx - 1,)), dma((n_ctx - 1,)), dma((n_ctx - 1,)),
        ],
        compiler_params=pltpu.CompilerParams(
            collective_id=0, has_side_effects=True, vmem_limit_bytes=60 << 20
        ),
    )(
        *(x.reshape(rows, width) for x in (query, key_in, value_in, cotangent)),
        filters,
        norm_gain.reshape(1, width),
    )
    outs = pl.pallas_call(
        store,
        out_shape=tuple(jax.ShapeDtypeStruct(x.shape, x.dtype) for x in outs),
        in_specs=[hbm] * 5,
        out_specs=(hbm,) * 5,
        scratch_shapes=[*[pltpu.VMEM(x.shape, x.dtype) for x in outs], dma((5,)), dma((5,))],
        compiler_params=pltpu.CompilerParams(vmem_limit_bytes=60 << 20),
    )(*outs)
    grad_filters = outs[4] if own_sum else lax.psum(outs[4], "ctx")
    return tuple(x.reshape(1, rows, width) for x in outs[:4]) + (grad_filters,)


def solution(mesh):
    spread = P(None, "ctx", "chan")
    return jax.shard_map(
        functools.partial(body, mesh.shape["ctx"], mesh.shape["chan"]),
        mesh=mesh,
        in_specs=(spread,) * 4 + (P("chan", None), P("chan")),
        out_specs=(spread,) * 4 + (P("chan", None),),
        check_vma=False,
    )
```

time: 55.8 us -> 47 us (0.84)
  local copies, waits for them, and re-layouts: 9.5 us -> 0 us
  Pallas kernels: 45.3 us -> 46.2 us
    unnamed x17 -> x0, local copies, waits for them, and re-layouts: 9.5 us -> none
    pallas_call x0 -> x1, Pallas kernels: none -> 2.45 us  [body(): pl.pallas_call(store, out_shape=tuple((jax.ShapeDtypeStruct(x.shape, x.dt...]
    pallas_call x1, Pallas kernels: 45.3 us -> 43.7 us  [body(): pl.pallas_call(functools.partial(kernel, n_ctx, n_chan, members, own_sum)...]
where the time goes in v2:
time: 47 us; the launch traced here: 46.8 us
  Pallas kernels  46.2 us (98%)
  between operations  0.64 us (1%)
    pallas_call x1, Pallas kernels, body(): pl.pallas_call(functools.partial(kernel, n_ctx, n_chan, members, own_sum)...  43.7 us
    pallas_call x1, Pallas kernels, body(): pl.pallas_call(store, out_shape=tuple((jax.ShapeDtypeStruct(x.shape, x.dt...  2.45 us

profile of v2, /device:TPU:0, one launch (start us, length us, event | category | flops | bytes accessed | tf_op | source)
XLA Modules:
  0.0 46.8 jit_solution(12367846662496963961)
XLA Ops:
  0.6 43.7 %shard_map.101 = (bf16[128,2048]{1,0:T(8,128)(2,1)}, bf16[128,2048]{1,0:T(8,128)(2,1)}, bf16[128,2048]{1,0:T(8,128)(2,1)}, bf16[128,2048]{1,0:T(8,128)(2,1)}, f32[128,128]{1,0:T(8,128)}) custom-call(bf16[128,2048]{1,0:T(8,128)(2,1)} %bitcast.9, bf16[128,2048]{1,0:T(8,128)(2,1)} %bitcast.10, bf16[128,2048]{1,0:T(8,128)(2,1)} %bitcast.11, ...), custom_call_target="tpu_custom_call" | custom-call | tf_op jit(solution)/shard_map/pallas_call | solution.py:329
  44.4 2.4 %shard_map.102 = (bf16[128,2048]{1,0:T(8,128)(2,1)}, bf16[128,2048]{1,0:T(8,128)(2,1)}, bf16[128,2048]{1,0:T(8,128)(2,1)}, bf16[128,2048]{1,0:T(8,128)(2,1)}, f32[128,128]{1,0:T(8,128)}) custom-call(bf16[128,2048]{1,0:T(8,128)(2,1)} %get-tuple-element.15.refs_0_, bf16[128,2048]{1,0:T(8,128)(2,1)} %get-tuple-element.16.refs_1_, ...), custom_call_target="tpu_custom_call" | custom-call | tf_op jit(solution)/shard_map/pallas_call | solution.py:366

commit v3 on v2

--- a/solution.py
+++ b/solution.py
@@ -104,7 +104,7 @@
     negate = (lax.rem(row + col, rows) == 0).astype(f32).astype(bf16)
     frev[...] = jnp.dot(taps_b, negate, preferred_element_type=f32)
 
-    @pl.loop(0, groups)
+    @pl.loop(0, groups, unroll=8)
     def _(g):
         at = pl.ds(pl.multiple_of(g * rows, rows), rows)
         turned = jnp.broadcast_to(frev[pl.ds(g, 1), :], (rows, rows))

time: 47 us -> 45.3 us (0.964)
  Pallas kernels: 46.2 us -> 44.5 us
    pallas_call x1, Pallas kernels: 43.7 us -> 42 us  [body(): pl.pallas_call(functools.partial(kernel, n_ctx, n_chan, members, own_sum)...]
where the time goes in v3:
time: 45.3 us; the launch traced here: 45.1 us
  Pallas kernels  44.5 us (98%)
  between operations  0.64 us (1%)
    pallas_call x1, Pallas kernels, body(): pl.pallas_call(functools.partial(kernel, n_ctx, n_chan, members, own_sum)...  42 us
    pallas_call x1, Pallas kernels, body(): pl.pallas_call(store, out_shape=tuple((jax.ShapeDtypeStruct(x.shape, x.dt...  2.45 us

profile of v3, /device:TPU:0, one launch (start us, length us, event | category | flops | bytes accessed | tf_op | source)
XLA Modules:
  0.0 45.1 jit_solution(17713906250735174811)
XLA Ops:
  0.6 42.0 %shard_map.101 = (bf16[128,2048]{1,0:T(8,128)(2,1)}, bf16[128,2048]{1,0:T(8,128)(2,1)}, bf16[128,2048]{1,0:T(8,128)(2,1)}, bf16[128,2048]{1,0:T(8,128)(2,1)}, f32[128,128]{1,0:T(8,128)}) custom-call(bf16[128,2048]{1,0:T(8,128)(2,1)} %bitcast.9, bf16[128,2048]{1,0:T(8,128)(2,1)} %bitcast.10, bf16[128,2048]{1,0:T(8,128)(2,1)} %bitcast.11, ...), custom_call_target="tpu_custom_call" | custom-call | tf_op jit(solution)/shard_map/pallas_call | solution.py:329
  42.7 2.4 %shard_map.102 = (bf16[128,2048]{1,0:T(8,128)(2,1)}, bf16[128,2048]{1,0:T(8,128)(2,1)}, bf16[128,2048]{1,0:T(8,128)(2,1)}, bf16[128,2048]{1,0:T(8,128)(2,1)}, f32[128,128]{1,0:T(8,128)}) custom-call(bf16[128,2048]{1,0:T(8,128)(2,1)} %get-tuple-element.15.refs_0_, bf16[128,2048]{1,0:T(8,128)(2,1)} %get-tuple-element.16.refs_1_, ...), custom_call_target="tpu_custom_call" | custom-call | tf_op jit(solution)/shard_map/pallas_call | solution.py:366

commit v4 on v3

--- a/solution.py
+++ b/solution.py
@@ -22,7 +22,7 @@
     normed_hbm, gq_hbm, gk_hbm, gv_hbm, gf_hbm,
     normed_ref, gq_ref, gk_ref, gv_ref, gf_ref, out_sem, gk_sem, gv_sem,
     q_ref, k_ref, v_ref, ct_ref, f_ref, gain_ref, in_sem,
-    win, gwin, srev, own, fwd, frev, mixed, power, inner, stats, part, land,
+    win, gwin, srev, own, fwd, frev, mixed, power, inner, stats, part, sent, land,
     sig_send, sig_recv, gc_send, gc_recv, st_send, st_recv, rs_send, rs_recv, ag_send, ag_recv,
 ):
     f32, bf16 = jnp.float32, jnp.bfloat16
@@ -211,7 +211,7 @@
     def scatter_copy(d):
         peer = ctx_peer(d)
         return pltpu.make_async_remote_copy(
-            src_ref=part.at[pl.ds(pl.multiple_of(peer * per, per), per), :],
+            src_ref=sent.at[pl.ds(pl.multiple_of(peer * per, per), per), :],
             dst_ref=land.at[d],
             send_sem=rs_send.at[d], recv_sem=rs_recv.at[d],
             device_id=(peer, chan), device_id_type=MESH,
@@ -239,6 +239,9 @@
             both = pltpu.roll(both, 1, 1, stride=1, stride_axis=0)
             part[pl.ds(c * per + k, 1), :] = jnp.sum(both, axis=0, keepdims=True)
         if own_sum:
+            at = pl.ds(pl.multiple_of(c * per, per), per)
+            sent[at, :] = part[at, :].astype(bf16)
+        if own_sum:
             @pl.when(i < nb - 1)
             def _():
                 scatter_copy(i).start()
@@ -266,7 +269,7 @@
         for d in range(n_ctx - 1):
             scatter_copy(d).wait_recv()
         at = pl.ds(pl.multiple_of(me * per, per), per)
-        gf_ref[at, :] = part[at, :] + jnp.sum(land[...], axis=0)
+        gf_ref[at, :] = part[at, :] + jnp.sum(land[...].astype(f32), axis=0)
         for d in range(n_ctx - 1):
             gather_copy(d, me).start()
     else:
@@ -350,7 +353,8 @@
             pltpu.VMEM((rows, rows), f32),
             pltpu.VMEM((n_chan, 8, rows), f32),
             pltpu.VMEM((groups, taps), f32),
-            pltpu.VMEM((n_ctx - 1, LANES // members, taps), f32),
+            pltpu.VMEM((groups, taps), bf16),
+            pltpu.VMEM((n_ctx - 1, LANES // members, taps), bf16),
             dma((nb,)), dma((nb,)), dma((nb,)), dma((nb,)),
             dma((n_chan - 1,)), dma((n_chan - 1,)),
             dma((n_ctx - 1,)), dma((n_ctx - 1,)), dma((n_ctx - 1,)), dma((n_ctx - 1,)),

time: 45.3 us -> 44.6 us (0.985)
  Pallas kernels: 44.5 us -> 43.8 us
    pallas_call x1, Pallas kernels: 42 us -> 41.4 us  [body(): pl.pallas_call(functools.partial(kernel, n_ctx, n_chan, members, own_sum)...]
where the time goes in v4:
time: 44.6 us; the launch traced here: 44.4 us
  Pallas kernels  43.8 us (98%)
  between operations  0.64 us (1%)
    pallas_call x1, Pallas kernels, body(): pl.pallas_call(functools.partial(kernel, n_ctx, n_chan, members, own_sum)...  41.4 us
    pallas_call x1, Pallas kernels, body(): pl.pallas_call(store, out_shape=tuple((jax.ShapeDtypeStruct(x.shape, x.dt...  2.45 us

profile of v4, /device:TPU:0, one launch (start us, length us, event | category | flops | bytes accessed | tf_op | source)
XLA Modules:
  0.0 44.4 jit_solution(17427653592728691011)
XLA Ops:
  0.6 41.4 %shard_map.101 = (bf16[128,2048]{1,0:T(8,128)(2,1)}, bf16[128,2048]{1,0:T(8,128)(2,1)}, bf16[128,2048]{1,0:T(8,128)(2,1)}, bf16[128,2048]{1,0:T(8,128)(2,1)}, f32[128,128]{1,0:T(8,128)}) custom-call(bf16[128,2048]{1,0:T(8,128)(2,1)} %bitcast.9, bf16[128,2048]{1,0:T(8,128)(2,1)} %bitcast.10, bf16[128,2048]{1,0:T(8,128)(2,1)} %bitcast.11, ...), custom_call_target="tpu_custom_call" | custom-call | tf_op jit(solution)/shard_map/pallas_call | solution.py:332
  42.0 2.4 %shard_map.102 = (bf16[128,2048]{1,0:T(8,128)(2,1)}, bf16[128,2048]{1,0:T(8,128)(2,1)}, bf16[128,2048]{1,0:T(8,128)(2,1)}, bf16[128,2048]{1,0:T(8,128)(2,1)}, f32[128,128]{1,0:T(8,128)}) custom-call(bf16[128,2048]{1,0:T(8,128)(2,1)} %get-tuple-element.15.refs_0_, bf16[128,2048]{1,0:T(8,128)(2,1)} %get-tuple-element.16.refs_1_, ...), custom_call_target="tpu_custom_call" | custom-call | tf_op jit(solution)/shard_map/pallas_call | solution.py:370
